TPU v7x, 32 devices: a whole 2x2x4 slice. The times are simulated.
32 devices in a mesh: group: 4 (over y, core), dev: 8 (over z, x).
Axes of the slice: x: 2, y: 2, z: 4, core: 2. Of those that a mesh axis runs over, the one named last changes fastest.
Arguments:
- node_state: bfloat16 [16384, 512], P(('group', 'dev')), may hold values from -6 to 6
- hub_state: bfloat16 [64, 512], P('dev'), may hold values from -6 to 6
- w_edge_in: bfloat16 [512, 256], replicated, may hold values from -0.25 to 0.25
- w_edge_out: bfloat16 [256, 512], replicated, may hold values from -0.375 to 0.375
- w_update: bfloat16 [512, 512], replicated, may hold values from -0.25 to 0.25
- edge_src: int32 [131072], P(('group', 'dev')), may hold values from 0 to 319
- edge_dst: int32 [131072], P(('group', 'dev')), may hold values from 0 to 319
- edge_mask: int32 [131072], P(('group', 'dev')), may hold values 0 or 1
- send_list: int32 [32, 8, 32], P(('group', 'dev')), may hold values from 0 to 511
- send_count: int32 [32, 8], P(('group', 'dev')), may hold values from 8 to 32, as said below
- node_cot: bfloat16 [16384, 512], P(('group', 'dev')), may hold values from -0.059814453 to 0.059814453
- hub_cot: bfloat16 [64, 512], P('dev'), may hold values from -0.059814453 to 0.059814453
Outputs:
- new_state: bfloat16 [16384, 512], P(('group', 'dev'))
- new_hub: bfloat16 [64, 512], P('dev')
- grad_in: float32 [512, 256], replicated
- grad_out: float32 [256, 512], replicated
- grad_update: float32 [512, 512], replicated
Inputs may be any that keep to these rules, and one draw needn't show every extreme that they name: Device 0 sends 32 live slots to peer 0: send_count[0, 0] = 32.
All inputs are finite; a program needn't handle non-finite values. No bound on the sum of `edge_mask` on one device may be relied on, other than what follows from the above.
Results may differ from a plain program's by a relative error of at most 0.0064.
The roundings to bfloat16 on the way count: a program that leaves them out, or rounds other values in their place, can miss the bound.
Values may be sent and summed in bfloat16 or wider, within the bound.
No kernel may reach another device: no remote copies, remote signals or barrier semaphores. Data moves between devices by JAX's collectives and lax.ppermute only.
A program may use at most 64 MiB of HBM per device.

v0:
```python
import jax
import jax.numpy as jnp
from jax import lax
from jax.sharding import PartitionSpec as P


def silu_grad(values):
    sigmoid_v = jax.nn.sigmoid(values)
    return sigmoid_v * (1.0 + values * (1.0 - sigmoid_v))


def finish(states, summed, degree, w_update):
    mean_part = summed / jnp.maximum(degree, 1.0)[:, None]
    mixed_rows = (states.astype(jnp.float32) + mean_part).astype(jnp.bfloat16)
    pre_update = jnp.dot(mixed_rows, w_update, preferred_element_type=jnp.float32)
    updated = (states.astype(jnp.float32) + jax.nn.silu(pre_update)).astype(jnp.bfloat16)
    return (mixed_rows, pre_update, updated)


def backward_rows(cotangent, pre_update, degree, w_update):
    grad_pre = (cotangent.astype(jnp.float32) * silu_grad(pre_update)).astype(jnp.bfloat16)
    grad_mix = jnp.dot(grad_pre, w_update.T, preferred_element_type=jnp.float32)
    grad_sum = (grad_mix / jnp.maximum(degree, 1.0)[:, None]).astype(jnp.bfloat16)
    return (grad_pre, grad_sum)


def shards(
    node_state,
    hub_state,
    w_edge_in,
    w_edge_out,
    w_update,
    edge_src,
    edge_dst,
    edge_mask,
    send_list,
    send_count,
    node_cot,
    hub_cot,
):
    width = node_state.shape[1]
    master_rows = node_state.shape[0]
    send_rows = send_list[0]
    peer_total = send_rows.shape[0]
    slot_width = send_rows.shape[1]
    mirror_total = peer_total * slot_width
    live_slot = jnp.arange(slot_width)[None, :] < send_count[0][:, None]
    flat_rows = send_rows.reshape(-1)
    flat_live = live_slot.reshape(-1)
    selector = (
        (flat_rows[:, None] == jnp.arange(master_rows)[None, :]) & flat_live[:, None]
    ).astype(jnp.bfloat16)
    contract = (((0,), (0,)), ((), ()))
    outgoing = jnp.dot(selector, node_state, preferred_element_type=jnp.float32).astype(
        jnp.bfloat16
    )
    mirror_rows = lax.all_to_all(
        outgoing.reshape(peer_total, slot_width, width),
        "dev",
        split_axis=0,
        concat_axis=0,
        tiled=True,
    )
    hub_table = lax.all_gather(hub_state, "dev", axis=0, tiled=True)
    local_table = jnp.concatenate([mirror_rows.reshape(mirror_total, width), hub_table], axis=0)
    local_rows = local_table.shape[0]
    edge_total = edge_src.shape[0]
    block_size = min(1024, edge_total)
    block_count = edge_total // block_size
    sources = edge_src.reshape(block_count, block_size)
    targets = edge_dst.reshape(block_count, block_size)
    edge_keep = edge_mask.reshape(block_count, block_size)
    row_ids = jnp.arange(local_rows)[None, :]

    def forward_step(totals, pieces):
        source_ids, target_ids, keep_ids = pieces
        gathered = local_table[source_ids]
        pre_act = jnp.dot(gathered, w_edge_in, preferred_element_type=jnp.float32)
        hidden = jax.nn.silu(pre_act).astype(jnp.bfloat16)
        message = jnp.dot(hidden, w_edge_out, preferred_element_type=jnp.float32).astype(
            jnp.bfloat16
        )
        onehot = ((target_ids[:, None] == row_ids) & (keep_ids[:, None] > 0)).astype(jnp.bfloat16)
        added = lax.dot_general(onehot, message, contract, preferred_element_type=jnp.float32)
        tally = jnp.sum(onehot, axis=0, dtype=jnp.float32)
        return ((totals[0] + added, totals[1] + tally), pre_act)

    start_fwd = (jnp.zeros((local_rows, width), jnp.float32), jnp.zeros((local_rows,), jnp.float32))
    (partial_value, counts_local), saved_acts = lax.scan(
        forward_step, start_fwd, (sources, targets, edge_keep)
    )
    mirror_part = (
        partial_value[:mirror_total].reshape(peer_total, slot_width, width).astype(jnp.bfloat16)
    )
    mirror_count = counts_local[:mirror_total].reshape(peer_total, slot_width).astype(jnp.bfloat16)
    back_part, back_count = (
        lax.all_to_all(mirror_part, "dev", split_axis=0, concat_axis=0, tiled=True),
        lax.all_to_all(mirror_count, "dev", split_axis=0, concat_axis=0, tiled=True),
    )
    summed = lax.dot_general(
        selector,
        back_part.reshape(mirror_total, width),
        contract,
        preferred_element_type=jnp.float32,
    )
    degree = lax.dot_general(
        selector, back_count.reshape(mirror_total, 1), contract, preferred_element_type=jnp.float32
    )[:, 0]
    hub_part = partial_value[mirror_total:]
    hub_count = counts_local[mirror_total:]
    whole_part, whole_count = (
        lax.psum(hub_part.astype(jnp.bfloat16), "group").astype(jnp.float32),
        lax.psum(hub_count.astype(jnp.bfloat16), "group").astype(jnp.float32),
    )
    hub_summed, hub_degree = (
        lax.psum_scatter(
            whole_part.astype(jnp.bfloat16), "dev", scatter_dimension=0, tiled=True
        ).astype(jnp.float32),
        lax.psum_scatter(
            whole_count.astype(jnp.bfloat16), "dev", scatter_dimension=0, tiled=True
        ).astype(jnp.float32),
    )
    mixed_rows, pre_update, new_state = finish(node_state, summed, degree, w_update)
    hub_mixed, hub_pre, new_hub = finish(hub_state, hub_summed, hub_degree, w_update)
    grad_pre, grad_sum = backward_rows(node_cot, pre_update, degree, w_update)
    hub_grad_pre, hub_grad_sum = backward_rows(hub_cot, hub_pre, hub_degree, w_update)
    grad_outgoing = jnp.dot(selector, grad_sum, preferred_element_type=jnp.float32).astype(
        jnp.bfloat16
    )
    grad_mirror = lax.all_to_all(
        grad_outgoing.reshape(peer_total, slot_width, width),
        "dev",
        split_axis=0,
        concat_axis=0,
        tiled=True,
    )
    grad_hubs = lax.all_gather(hub_grad_sum, "dev", axis=0, tiled=True)
    grad_table = jnp.concatenate([grad_mirror.reshape(mirror_total, width), grad_hubs], axis=0)
    hub_weight = (lax.axis_index("group") == 0).astype(jnp.float32)
    grad_update = lax.dot_general(
        mixed_rows, grad_pre, contract, preferred_element_type=jnp.float32
    )
    grad_update = grad_update + hub_weight * lax.dot_general(
        hub_mixed, hub_grad_pre, contract, preferred_element_type=jnp.float32
    )

    def backward_step(totals, pieces):
        source_ids, target_ids, keep_ids, pre_act = pieces
        gathered = local_table[source_ids]
        hidden = jax.nn.silu(pre_act).astype(jnp.bfloat16)
        grad_message = jnp.where(
            keep_ids[:, None] > 0, grad_table[target_ids], jnp.zeros((), jnp.bfloat16)
        )
        grad_w_out = lax.dot_general(
            hidden, grad_message, contract, preferred_element_type=jnp.float32
        )
        grad_hidden = jnp.dot(grad_message, w_edge_out.T, preferred_element_type=jnp.float32)
        grad_act = (grad_hidden * silu_grad(pre_act)).astype(jnp.bfloat16)
        grad_w_in = lax.dot_general(
            gathered, grad_act, contract, preferred_element_type=jnp.float32
        )
        return ((totals[0] + grad_w_in, totals[1] + grad_w_out), None)

    start = (jnp.zeros(w_edge_in.shape, jnp.float32), jnp.zeros(w_edge_out.shape, jnp.float32))
    local_grads, _ = lax.scan(backward_step, start, (sources, targets, edge_keep, saved_acts))
    grad_in, grad_out, grad_upd = lax.psum(
        (local_grads[0], local_grads[1], grad_update), ("group", "dev")
    )
    return (new_state, new_hub, grad_in, grad_out, grad_upd)


def solution(mesh):
    return jax.shard_map(
        shards,
        mesh=mesh,
        in_specs=(
            P(("group", "dev"), None),
            P("dev", None),
            P(),
            P(),
            P(),
            P(("group", "dev")),
            P(("group", "dev")),
            P(("group", "dev")),
            P(("group", "dev"), None, None),
            P(("group", "dev"), None),
            P(("group", "dev"), None),
            P("dev", None),
        ),
        out_specs=(P(("group", "dev"), None), P("dev", None), P(), P(), P()),
        check_vma=False,
    )
```

profile of v0, /device:TPU:0, one launch (start us, length us, event | category | flops | bytes accessed | tf_op | source)
XLA Modules:
  0.0 417.0 jit_solution(8544541724577750692)
XLA Ops:
  10.9 7.2 %all-to-all-start = ((bf16[8,32,512]{2,1,0:T(8,128)(2,1)}), bf16[8,32,512]{2,1,0:T(8,128)(2,1)S(1)}, u32[]{:S(2)}, u32[]{:S(2)}) async-start(bf16[8,32,512]{2,1,0:T(8,128)(2,1)} %bitcast.1), calls=%async_computation | async-start | bytes 524288 | tf_op jit(solution)/shard_map/all_to_all | solution.py:57
  20.4 31.2 %all_gather.6 = bf16[64,512]{1,0:T(8,128)(2,1)S(1)} all-gather(bf16[8,512]{1,0:T(8,128)(2,1)} %param.17), channel_id=1, replica_groups=mesh['group'=4,'dev'=8] {'dev'}, dimensions={0}, use_global_device_ids=true | all-gather | bytes 73728 | tf_op jit(solution)/shard_map/all_gather | solution.py:64
  51.7 33.4 %while.28 = (s32[]{:T(128)}, f32[320,512]{1,0:T(8,128)}, f32[320]{0:T(512)S(1)}, f32[4,1024,256]{2,1,0:T(8,128)}, s32[4,1024]{1,0:T(4,128)S(1)}, /*index=5*/s32[...) while((s32[]{:T(128)}, f32[320,512]{1,0:T(8,128)}, ...), condition=%wide.region_2.3_spmd.clone, body=%wide.region_0.2_spmd.clone.sunk | while | flops 876877120 | bytes 10273476 | solution.py:89
  51.8 4.0 gather_fusion
  59.3 4.0 gather_fusion
  67.9 4.0 gather_fusion
  76.5 4.0 gather_fusion
  85.8 5.4 %all-to-all-start.2 = ((bf16[8,1,32]{2,1,0:T(2,128)(2,1)}), bf16[8,1,32]{2,1,0:T(2,128)(2,1)S(1)}, u32[]{:S(2)}, u32[]{:S(2)}) async-start(bf16[8,1,32]{2,1,0:T(2,128)(2,1)} %convert_element_type.118), calls=%async_computation.2 | async-start | bytes 8192 | tf_op jit(solution)/shard_map/all_to_all | solution.py:98
  95.1 21.8 %all-reduce = bf16[64]{0:T(256)(128)(2,1)S(1)} all-reduce(bf16[64]{0:T(256)(128)(2,1)S(1)} %slice.27), channel_id=3, replica_groups=mesh['group'=4,'dev'=8] {'dev'}, use_global_device_ids=true, to_apply=%region_6.7.clone | all-reduce | flops 64 | bytes 256
  120.8 38.2 %reduce-scatter.2.cloned.1.call-done = bf16[8,512]{1,0:T(8,128)(2,1)} async-done(((bf16[64,512]{1,0:T(8,128)(2,1)}), bf16[8,512]{1,0:T(8,128)(2,1)}) %reduce-scatter.2.cloned.1.call-update) | async-done | bytes 8208 | tf_op jit(solution)/shard_map/reduce_scatter | solution.py:116
  159.0 6.0 %all-reduce.2 = (bf16[8,512]{1,0:T(8,128)(2,1)S(1)}, bf16[8]{0:T(256)(128)(2,1)S(1)}) all-reduce(bf16[8,512]{1,0:T(8,128)(2,1)} %reduce-scatter.2.cloned.1.call-done, bf16[8]{0:T(256)(128)(2,1)S(1)} %dynamic-slice.1), channel_id=1, replica_groups=mesh['group'=4,'dev'=8] {'group'}, use_global_device_ids=true, to_apply=%region_3.4 | all-reduce | flops 4104 | bytes 16416 | tf_op jit(solution)/shard_map/psum | solution.py:112
  166.1 30.5 %all_gather.7 = bf16[64,512]{1,0:T(8,128)(2,1)S(1)} all-gather(bf16[8,512]{1,0:T(8,128)(2,1)S(1)} %fusion.42), channel_id=1, replica_groups=mesh['group'=4,'dev'=8] {'dev'}, dimensions={0}, use_global_device_ids=true | all-gather | bytes 73728 | tf_op jit(solution)/shard_map/all_gather | solution.py:137
  202.3 3.6 all-to-all-start.3
  207.8 6.3 %all-to-all-done.3 = bf16[8,32,512]{2,1,0:T(8,128)(2,1)S(1)} async-done(((bf16[8,32,512]{2,1,0:T(8,128)(2,1)}), bf16[8,32,512]{2,1,0:T(8,128)(2,1)S(1)}, u32[]{:S(2)}, u32[]{:S(2)}) %all-to-all-start.3) | async-done | bytes 262176 | tf_op jit(solution)/shard_map/all_to_all | solution.py:130
  214.1 56.7 %while.29 = (s32[]{:T(128)}, f32[512,256]{1,0:T(8,128)}, f32[256,512]{1,0:T(8,128)}, s32[4,1024]{1,0:T(4,128)S(1)}, bf16[320,512]{1,0:T(8,128)(2,1)S(1)}, /*inde...) while((s32[]{:T(128)}, f32[512,256]{1,0:T(8,128)}, ...), condition=%wide.region_8.9_spmd.clone, body=%wide.region_7.8_spmd.clone.sunk | while | flops 810558464 | bytes 11845768 | solution.py:165
  214.2 4.0 gather_fusion.2
  218.2 4.0 gather_fusion.1
  228.1 4.0 gather_fusion.2
  232.1 4.0 gather_fusion.1
  242.4 4.0 gather_fusion.2
  246.3 4.0 gather_fusion.1
  256.6 4.0 gather_fusion.2
  260.6 4.0 gather_fusion.1
  270.8 133.3 %all-reduce.5.cloned.1.call-done = (f32[512,256]{1,0:T(8,128)}, f32[256,512]{1,0:T(8,128)}, f32[512,512]{1,0:T(8,128)}) async-done(((f32[512,256]{1,0:T(8,128)}, f32[256,512]{1,0:T(8,128)}, f32[512,512]{1,0:T(8,128)}), (f32[512,256]{1,0:T(8,128)}, f32[256,512]{1,0:T(8,128)}, f32[512,512]{1,0:T(8,128)})) %all-reduce.5.cloned.1.call-update) | async-done | bytes 2097168 | tf_op jit(solution)/shard_map/psum | solution.py:166
  (128 shorter events, 70.4 us)
Async XLA Ops:
  7.2 157.8 %copy-start = (bf16[512,512]{1,0:T(8,128)(2,1)S(1)}, bf16[512,512]{1,0:T(8,128)(2,1)}, u32[]{:S(2)}) copy-start(bf16[512,512]{1,0:T(8,128)(2,1)} %param.20) | copy-start | bytes 1572868
  10.9 40.7 %all-to-all-start = ((bf16[8,32,512]{2,1,0:T(8,128)(2,1)}), bf16[8,32,512]{2,1,0:T(8,128)(2,1)S(1)}, u32[]{:S(2)}, u32[]{:S(2)}) async-start(bf16[8,32,512]{2,1,0:T(8,128)(2,1)} %bitcast.1), calls=%async_computation | async-start | bytes 524288 | tf_op jit(solution)/shard_map/all_to_all | solution.py:57
  51.7 39.6 %copy-start.6 = (u32[32]{0:T(128)S(1)}, u32[32]{0:T(128)}, u32[]{:S(2)}) copy-start(u32[32]{0:T(128)} %constant.65) | copy-start | bytes 388
  51.7 113.3 %copy-start.2 = (bf16[8,512]{1,0:T(8,128)(2,1)S(1)}, bf16[8,512]{1,0:T(8,128)(2,1)}, u32[]{:S(2)}) copy-start(bf16[8,512]{1,0:T(8,128)(2,1)} %param.17) | copy-start | bytes 24580
  51.7 114.2 %copy-start.3 = (bf16[8,512]{1,0:T(8,128)(2,1)S(1)}, bf16[8,512]{1,0:T(8,128)(2,1)}, u32[]{:S(2)}) copy-start(bf16[8,512]{1,0:T(8,128)(2,1)} %param.27) | copy-start | bytes 24580
  51.7 4.0 copy-start.1
  51.8 5.5 %copy-start.5 = (bf16[256,512]{1,0:T(8,128)(2,1)S(1)}, bf16[256,512]{1,0:T(8,128)(2,1)}, u32[]{:S(2)}) copy-start(bf16[256,512]{1,0:T(8,128)(2,1)} %get-tuple-element.406) | copy-start | bytes 786436 | tf_op jit(solution)/shard_map/while
  59.2 4.0 copy-start.1
  59.3 5.5 %copy-start.5 = (bf16[256,512]{1,0:T(8,128)(2,1)S(1)}, bf16[256,512]{1,0:T(8,128)(2,1)}, u32[]{:S(2)}) copy-start(bf16[256,512]{1,0:T(8,128)(2,1)} %get-tuple-element.406) | copy-start | bytes 786436 | tf_op jit(solution)/shard_map/while
  67.9 4.0 copy-start.1
  67.9 5.5 %copy-start.5 = (bf16[256,512]{1,0:T(8,128)(2,1)S(1)}, bf16[256,512]{1,0:T(8,128)(2,1)}, u32[]{:S(2)}) copy-start(bf16[256,512]{1,0:T(8,128)(2,1)} %get-tuple-element.406) | copy-start | bytes 786436 | tf_op jit(solution)/shard_map/while
  76.5 4.0 copy-start.1
  76.5 5.5 %copy-start.5 = (bf16[256,512]{1,0:T(8,128)(2,1)S(1)}, bf16[256,512]{1,0:T(8,128)(2,1)}, u32[]{:S(2)}) copy-start(bf16[256,512]{1,0:T(8,128)(2,1)} %get-tuple-element.406) | copy-start | bytes 786436 | tf_op jit(solution)/shard_map/while
  85.8 31.2 %all-to-all-start.2 = ((bf16[8,1,32]{2,1,0:T(2,128)(2,1)}), bf16[8,1,32]{2,1,0:T(2,128)(2,1)S(1)}, u32[]{:S(2)}, u32[]{:S(2)}) async-start(bf16[8,1,32]{2,1,0:T(2,128)(2,1)} %convert_element_type.118), calls=%async_computation.2 | async-start | bytes 8192 | tf_op jit(solution)/shard_map/all_to_all | solution.py:98
  91.2 67.8 %reduce-scatter.2.cloned.1.call-start = ((), (), s32[]{:S(2)}) async-start(), calls=%async_computation.5 | async-start | bytes 73728 | tf_op jit(solution)/shard_map/reduce_scatter | solution.py:116
  92.5 105.6 %copy-start.4 = (bf16[512,512]{1,0:T(8,128)(2,1)S(1)}, bf16[512,512]{1,0:T(8,128)(2,1)}, u32[]{:S(2)}) copy-start(bf16[512,512]{1,0:T(8,128)(2,1)} %param.26) | copy-start | bytes 1572868
  117.0 79.6 %all-to-all-start.1 = ((bf16[8,32,512]{2,1,0:T(8,128)(2,1)}), bf16[8,32,512]{2,1,0:T(8,128)(2,1)S(1)}, u32[]{:S(2)}, u32[]{:S(2)}) async-start(bf16[8,32,512]{2,1,0:T(8,128)(2,1)} %bitcast.3), calls=%async_computation.1 | async-start | bytes 524288 | tf_op jit(solution)/shard_map/all_to_all | solution.py:97
  202.3 11.8 %all-to-all-start.3 = ((bf16[8,32,512]{2,1,0:T(8,128)(2,1)}), bf16[8,32,512]{2,1,0:T(8,128)(2,1)S(1)}, u32[]{:S(2)}, u32[]{:S(2)}) async-start(bf16[8,32,512]{2,1,0:T(8,128)(2,1)} %bitcast.6), calls=%async_computation.3 | async-start | bytes 524288 | tf_op jit(solution)/shard_map/all_to_all | solution.py:130
  205.9 198.3 %all-reduce.5.cloned.1.call-start = ((), (), s32[]{:S(2)}) async-start(), calls=%async_computation.6 | async-start | bytes 4194304 | tf_op jit(solution)/shard_map/psum | solution.py:166
Sparse Core Ops, SparseCore 0:
  96.0 62.9 reduce-scatter.1
  270.9 133.1 all-reduce.4
where the time goes:
time: 418 us; the launch traced here: 417 us
  waiting for transfers between devices  178 us (43%)
  blocking collectives  89.5 us (21%)
  local copies, waits for them, and re-layouts  59.5 us (14%)
  matrix products  51.1 us (12%)
  starting transfers between devices  19.8 us (5%)
  between operations  14.9 us (4%)
    psum x1, waiting for transfers between devices, shards(): lax.psum((local_grads[0], local_grads[1], grad_update), ('group', 'dev'))  133 us
    reduce_scatter x1, waiting for transfers between devices, shards(): lax.psum_scatter(whole_part.astype(jnp.bfloat16), 'dev', scatter_dimensio...  38.2 us
    all_gather x1, blocking collectives, shards(): hub_table = lax.all_gather(hub_state, 'dev', axis=0, tiled=True)  31.2 us
    all_gather x1, blocking collectives, shards(): grad_hubs = lax.all_gather(hub_grad_sum, 'dev', axis=0, tiled=True)  30.5 us
    unnamed x1, blocking collectives  21.8 us
    gather x4, local copies, waits for them, and re-layouts, backward_step(): grad_table[target_ids]  15.9 us
    gather x4, local copies, waits for them, and re-layouts, backward_step(): gathered = local_table[source_ids]  15.9 us
    gather x4, local copies, waits for them, and re-layouts, forward_step(): gathered = local_table[source_ids]  15.9 us
  transfers between devices with their start and end apart: 6, of which 3 were waited for; matrix products, arithmetic and copies ran while one was open for 2% of the time, Pallas kernels for 0%

commit v1 on v0

--- a/solution.py
+++ b/solution.py
@@ -134,7 +134,24 @@
         concat_axis=0,
         tiled=True,
     )
-    grad_hubs = lax.all_gather(hub_grad_sum, "dev", axis=0, tiled=True)
+    size, index, rows = (lax.axis_size("dev"), lax.axis_index("dev"), hub_grad_sum.shape[0])
+    upward = [(i, (i + 1) % size) for i in range(size)]
+    backward = [(i, (i - 1) % size) for i in range(size)]
+    out = jnp.zeros(
+        (*hub_grad_sum.shape[:0], size * rows, *hub_grad_sum.shape[0 + 1 :]), hub_grad_sum.dtype
+    )
+    out = lax.dynamic_update_slice_in_dim(out, hub_grad_sum, index * rows, axis=0)
+    from_left = from_right = hub_grad_sum
+    halfway = size // 2
+    for hop in range(1, halfway + 1):
+        from_left = lax.ppermute(from_left, "dev", upward)
+        out = lax.dynamic_update_slice_in_dim(out, from_left, (index - hop) % size * rows, axis=0)
+        if hop < size - halfway:
+            from_right = lax.ppermute(from_right, "dev", backward)
+            out = lax.dynamic_update_slice_in_dim(
+                out, from_right, (index + hop) % size * rows, axis=0
+            )
+    grad_hubs = out
     grad_table = jnp.concatenate([grad_mirror.reshape(mirror_total, width), grad_hubs], axis=0)
     hub_weight = (lax.axis_index("group") == 0).astype(jnp.float32)
     grad_update = lax.dot_general(

time: 418 us -> 414 us (level)
  blocking collectives: 89.5 us -> 58.9 us
  starting transfers between devices: 19.8 us -> 33.8 us
  waiting for transfers between devices: 178 us -> 189 us
    all_gather x1 -> x0, blocking collectives: 30.5 us -> none  [shards(): grad_hubs = lax.all_gather(hub_grad_sum, 'dev', axis=0, tiled=True)]
    ppermute x0 -> x7, starting transfers between devices: none -> 14.2 us  [the longest x3 12.7 us: shards(): from_right = lax.ppermute(from_right, 'dev', backward)]
    ppermute x0 -> x7, waiting for transfers between devices: none -> 11.2 us  [the longest x4 11.2 us: shards(): from_left = lax.ppermute(from_left, 'dev', upward)]
  transfers between devices with their start and end apart: 6 -> 13, of which waited for: 3 -> 7; matrix products, arithmetic and copies ran while one was open for 2% -> 2% of each run, Pallas kernels for 0% -> 0%
where the time goes in v1:
time: 414 us; the launch traced here: 413 us
  waiting for transfers between devices  189 us (46%)
  local copies, waits for them, and re-layouts  60.3 us (15%)
  blocking collectives  58.9 us (14%)
  matrix products  51.2 us (12%)
  starting transfers between devices  33.8 us (8%)
  between operations  15.1 us (4%)
    psum x1, waiting for transfers between devices, shards(): lax.psum((local_grads[0], local_grads[1], grad_update), ('group', 'dev'))  133 us
    reduce_scatter x1, waiting for transfers between devices, shards(): lax.psum_scatter(whole_part.astype(jnp.bfloat16), 'dev', scatter_dimensio...  38.7 us
    all_gather x1, blocking collectives, shards(): hub_table = lax.all_gather(hub_state, 'dev', axis=0, tiled=True)  31.1 us
    unnamed x1, blocking collectives  21.8 us
    gather x4, local copies, waits for them, and re-layouts, backward_step(): grad_table[target_ids]  15.9 us
    gather x4, local copies, waits for them, and re-layouts, forward_step(): gathered = local_table[source_ids]  15.9 us
    gather x4, local copies, waits for them, and re-layouts, backward_step(): gathered = local_table[source_ids]  15.9 us
    dot_general x4, matrix products, backward_step(): lax.dot_general(gathered, grad_act, contract, preferred_element_type=jnp....  13.8 us
  transfers between devices with their start and end apart: 13, of which 7 were waited for; matrix products, arithmetic and copies ran while one was open for 2% of the time, Pallas kernels for 0%

profile of v1, /device:TPU:0, one launch (start us, length us, event | category | flops | bytes accessed | tf_op | source)
XLA Modules:
  0.0 413.0 jit_solution(1058595964766229551)
XLA Ops:
  10.9 7.2 %all-to-all-start = ((bf16[8,32,512]{2,1,0:T(8,128)(2,1)}), bf16[8,32,512]{2,1,0:T(8,128)(2,1)S(1)}, u32[]{:S(2)}, u32[]{:S(2)}) async-start(bf16[8,32,512]{2,1,0:T(8,128)(2,1)} %bitcast.1), calls=%async_computation | async-start | bytes 524288 | tf_op jit(solution)/shard_map/all_to_all | solution.py:57
  21.8 31.1 %all_gather.3 = bf16[64,512]{1,0:T(8,128)(2,1)S(1)} all-gather(bf16[8,512]{1,0:T(8,128)(2,1)} %param.17), channel_id=1, replica_groups=mesh['group'=4,'dev'=8] {'dev'}, dimensions={0}, use_global_device_ids=true | all-gather | bytes 73728 | tf_op jit(solution)/shard_map/all_gather | solution.py:64
  53.0 33.3 %while.28 = (s32[]{:T(128)}, f32[320,512]{1,0:T(8,128)}, f32[320]{0:T(512)S(1)}, f32[4,1024,256]{2,1,0:T(8,128)}, s32[4,1024]{1,0:T(4,128)S(1)}, /*index=5*/s32[...) while((s32[]{:T(128)}, f32[320,512]{1,0:T(8,128)}, ...), condition=%wide.region_2.3_spmd.clone, body=%wide.region_0.2_spmd.clone.sunk | while | flops 876877120 | bytes 10273476 | solution.py:89
  53.1 4.0 gather_fusion
  60.6 4.0 gather_fusion
  69.2 4.0 gather_fusion
  77.8 4.0 gather_fusion
  87.0 5.4 %all-to-all-start.2 = ((bf16[8,1,32]{2,1,0:T(2,128)(2,1)}), bf16[8,1,32]{2,1,0:T(2,128)(2,1)S(1)}, u32[]{:S(2)}, u32[]{:S(2)}) async-start(bf16[8,1,32]{2,1,0:T(2,128)(2,1)} %convert_element_type.118), calls=%async_computation.2 | async-start | bytes 8192 | tf_op jit(solution)/shard_map/all_to_all | solution.py:98
  95.8 21.8 %all-reduce = bf16[64]{0:T(256)(128)(2,1)S(1)} all-reduce(bf16[64]{0:T(256)(128)(2,1)S(1)} %slice.27), channel_id=3, replica_groups=mesh['group'=4,'dev'=8] {'dev'}, use_global_device_ids=true, to_apply=%region_6.7.clone | all-reduce | flops 64 | bytes 256
  121.5 38.7 %reduce-scatter.2.cloned.1.call-done = bf16[8,512]{1,0:T(8,128)(2,1)} async-done(((bf16[64,512]{1,0:T(8,128)(2,1)}), bf16[8,512]{1,0:T(8,128)(2,1)}) %reduce-scatter.2.cloned.1.call-update) | async-done | bytes 8208 | tf_op jit(solution)/shard_map/reduce_scatter | solution.py:116
  160.3 6.0 %all-reduce.2 = (bf16[8,512]{1,0:T(8,128)(2,1)S(1)}, bf16[8]{0:T(256)(128)(2,1)S(1)}) all-reduce(bf16[8,512]{1,0:T(8,128)(2,1)} %reduce-scatter.2.cloned.1.call-done, bf16[8]{0:T(256)(128)(2,1)S(1)} %dynamic-slice.1), channel_id=1, replica_groups=mesh['group'=4,'dev'=8] {'group'}, use_global_device_ids=true, to_apply=%region_3.4 | all-reduce | flops 4104 | bytes 16416 | tf_op jit(solution)/shard_map/psum | solution.py:112
  173.8 4.7 %collective-permute-start.3 = (bf16[8,512]{1,0:T(8,128)(2,1)S(1)}, bf16[8,512]{1,0:T(8,128)(2,1)S(1)}, u32[]{:S(2)}, u32[]{:S(2)}) collective-permute-start(bf16[8,512]{1,0:T(8,128)(2,1)S(1)} %collective-permute-done.1), channel_id=1, source_target_pairs={{0,7},{1,0},{2,1},{3,2},{4,3},{5,4},{6,5},{7,6},{8,15},{9,8},{10,9... | collective-permute-start | bytes 24584 | tf_op jit(solution)/shard_map/ppermute | solution.py:150
  180.1 4.7 %collective-permute-start.5 = (bf16[8,512]{1,0:T(8,128)(2,1)S(1)}, bf16[8,512]{1,0:T(8,128)(2,1)S(1)}, u32[]{:S(2)}, u32[]{:S(2)}) collective-permute-start(bf16[8,512]{1,0:T(8,128)(2,1)S(1)} %collective-permute-done.3), channel_id=1, source_target_pairs={{0,7},{1,0},{2,1},{3,2},{4,3},{5,4},{6,5},{7,6},{8,15},{9,8},{10,9... | collective-permute-start | bytes 24584 | tf_op jit(solution)/shard_map/ppermute | solution.py:150
  186.5 6.3 %collective-permute-done.6 = bf16[8,512]{1,0:T(8,128)(2,1)S(1)} collective-permute-done((bf16[8,512]{1,0:T(8,128)(2,1)S(1)}, bf16[8,512]{1,0:T(8,128)(2,1)S(1)}, u32[]{:S(2)}, u32[]{:S(2)}) %collective-permute-start.6) | collective-permute-done | bytes 8224 | tf_op jit(solution)/shard_map/ppermute | solution.py:147
  203.8 6.3 %all-to-all-done.3 = bf16[8,32,512]{2,1,0:T(8,128)(2,1)S(1)} async-done(((bf16[8,32,512]{2,1,0:T(8,128)(2,1)}), bf16[8,32,512]{2,1,0:T(8,128)(2,1)S(1)}, u32[]{:S(2)}, u32[]{:S(2)}) %all-to-all-start.3) | async-done | bytes 262176 | tf_op jit(solution)/shard_map/all_to_all | solution.py:130
  210.1 56.9 %while.29 = (s32[]{:T(128)}, f32[512,256]{1,0:T(8,128)}, f32[256,512]{1,0:T(8,128)}, s32[4,1024]{1,0:T(4,128)S(1)}, bf16[320,512]{1,0:T(8,128)(2,1)S(1)}, /*inde...) while((s32[]{:T(128)}, f32[512,256]{1,0:T(8,128)}, ...), condition=%wide.region_8.9_spmd.clone, body=%wide.region_7.8_spmd.clone.sunk | while | flops 810558464 | bytes 11845768 | solution.py:182
  210.1 4.0 gather_fusion.2
  214.1 4.0 gather_fusion.1
  224.1 4.0 gather_fusion.2
  228.1 4.0 gather_fusion.1
  238.4 4.0 gather_fusion.2
  242.4 4.0 gather_fusion.1
  252.7 4.0 gather_fusion.2
  267.0 133.2 %all-reduce.5.cloned.1.call-done = (f32[512,256]{1,0:T(8,128)}, f32[256,512]{1,0:T(8,128)}, f32[512,512]{1,0:T(8,128)}) async-done(((f32[512,256]{1,0:T(8,128)}, f32[256,512]{1,0:T(8,128)}, f32[512,512]{1,0:T(8,128)}), (f32[512,256]{1,0:T(8,128)}, f32[256,512]{1,0:T(8,128)}, f32[512,512]{1,0:T(8,128)})) %all-reduce.5.cloned.1.call-update) | async-done | bytes 2097168 | tf_op jit(solution)/shard_map/psum | solution.py:183
  (147 shorter events, 88.2 us)
Async XLA Ops:
  7.2 159.1 %copy-start = (bf16[512,512]{1,0:T(8,128)(2,1)S(1)}, bf16[512,512]{1,0:T(8,128)(2,1)}, u32[]{:S(2)}) copy-start(bf16[512,512]{1,0:T(8,128)(2,1)} %param.20) | copy-start | bytes 1572868
  10.9 42.0 %all-to-all-start = ((bf16[8,32,512]{2,1,0:T(8,128)(2,1)}), bf16[8,32,512]{2,1,0:T(8,128)(2,1)S(1)}, u32[]{:S(2)}, u32[]{:S(2)}) async-start(bf16[8,32,512]{2,1,0:T(8,128)(2,1)} %bitcast.1), calls=%async_computation | async-start | bytes 524288 | tf_op jit(solution)/shard_map/all_to_all | solution.py:57
  53.0 113.3 %copy-start.2 = (bf16[8,512]{1,0:T(8,128)(2,1)S(1)}, bf16[8,512]{1,0:T(8,128)(2,1)}, u32[]{:S(2)}) copy-start(bf16[8,512]{1,0:T(8,128)(2,1)} %param.17) | copy-start | bytes 24580
  53.0 114.2 %copy-start.3 = (bf16[8,512]{1,0:T(8,128)(2,1)S(1)}, bf16[8,512]{1,0:T(8,128)(2,1)}, u32[]{:S(2)}) copy-start(bf16[8,512]{1,0:T(8,128)(2,1)} %param.27) | copy-start | bytes 24580
  53.0 4.0 copy-start.1
  53.0 5.5 %copy-start.5 = (bf16[256,512]{1,0:T(8,128)(2,1)S(1)}, bf16[256,512]{1,0:T(8,128)(2,1)}, u32[]{:S(2)}) copy-start(bf16[256,512]{1,0:T(8,128)(2,1)} %get-tuple-element.408) | copy-start | bytes 786436 | tf_op jit(solution)/shard_map/while
  60.5 4.0 copy-start.1
  60.6 5.5 %copy-start.5 = (bf16[256,512]{1,0:T(8,128)(2,1)S(1)}, bf16[256,512]{1,0:T(8,128)(2,1)}, u32[]{:S(2)}) copy-start(bf16[256,512]{1,0:T(8,128)(2,1)} %get-tuple-element.408) | copy-start | bytes 786436 | tf_op jit(solution)/shard_map/while
  69.2 4.0 copy-start.1
  69.2 5.5 %copy-start.5 = (bf16[256,512]{1,0:T(8,128)(2,1)S(1)}, bf16[256,512]{1,0:T(8,128)(2,1)}, u32[]{:S(2)}) copy-start(bf16[256,512]{1,0:T(8,128)(2,1)} %get-tuple-element.408) | copy-start | bytes 786436 | tf_op jit(solution)/shard_map/while
  77.8 5.5 %copy-start.5 = (bf16[256,512]{1,0:T(8,128)(2,1)S(1)}, bf16[256,512]{1,0:T(8,128)(2,1)}, u32[]{:S(2)}) copy-start(bf16[256,512]{1,0:T(8,128)(2,1)} %get-tuple-element.408) | copy-start | bytes 786436 | tf_op jit(solution)/shard_map/while
  87.0 30.7 %all-to-all-start.2 = ((bf16[8,1,32]{2,1,0:T(2,128)(2,1)}), bf16[8,1,32]{2,1,0:T(2,128)(2,1)S(1)}, u32[]{:S(2)}, u32[]{:S(2)}) async-start(bf16[8,1,32]{2,1,0:T(2,128)(2,1)} %convert_element_type.118), calls=%async_computation.2 | async-start | bytes 8192 | tf_op jit(solution)/shard_map/all_to_all | solution.py:98
  92.4 67.8 %reduce-scatter.2.cloned.1.call-start = ((), (), s32[]{:S(2)}) async-start(), calls=%async_computation.5 | async-start | bytes 73728 | tf_op jit(solution)/shard_map/reduce_scatter | solution.py:116
  93.2 101.1 %copy-start.4 = (bf16[512,512]{1,0:T(8,128)(2,1)S(1)}, bf16[512,512]{1,0:T(8,128)(2,1)}, u32[]{:S(2)}) copy-start(bf16[512,512]{1,0:T(8,128)(2,1)} %param.26) | copy-start | bytes 1572868
  117.7 75.1 %all-to-all-start.1 = ((bf16[8,32,512]{2,1,0:T(8,128)(2,1)}), bf16[8,32,512]{2,1,0:T(8,128)(2,1)S(1)}, u32[]{:S(2)}, u32[]{:S(2)}) async-start(bf16[8,32,512]{2,1,0:T(8,128)(2,1)} %bitcast.3), calls=%async_computation.1 | async-start | bytes 524288 | tf_op jit(solution)/shard_map/all_to_all | solution.py:97
  167.4 6.4 %collective-permute-start = (bf16[8,512]{1,0:T(8,128)(2,1)S(1)}, bf16[8,512]{1,0:T(8,128)(2,1)S(1)}, u32[]{:S(2)}, u32[]{:S(2)}) collective-permute-start(bf16[8,512]{1,0:T(8,128)(2,1)S(1)} %get-tuple-element.244), channel_id=1, source_target_pairs={{0,1},{1,2},{2,3},{3,4},{4,5},{5,6},{6,7},{7,0},{8,9},{9,10},{10,1... | collective-permute-start | bytes 24584 | tf_op jit(solution)/shard_map/ppermute | solution.py:147
  168.8 4.9 %collective-permute-start.1 = (bf16[8,512]{1,0:T(8,128)(2,1)S(1)}, bf16[8,512]{1,0:T(8,128)(2,1)S(1)}, u32[]{:S(2)}, u32[]{:S(2)}) collective-permute-start(bf16[8,512]{1,0:T(8,128)(2,1)S(1)} %get-tuple-element.244), channel_id=1, source_target_pairs={{0,7},{1,0},{2,1},{3,2},{4,3},{5,4},{6,5},{7,6},{8,15},{9,8},{10,9... | collective-permute-start | bytes 24584 | tf_op jit(solution)/shard_map/ppermute | solution.py:150
  173.8 6.3 %collective-permute-start.2 = (bf16[8,512]{1,0:T(8,128)(2,1)S(1)}, bf16[8,512]{1,0:T(8,128)(2,1)S(1)}, u32[]{:S(2)}, u32[]{:S(2)}) collective-permute-start(bf16[8,512]{1,0:T(8,128)(2,1)S(1)} %collective-permute-done), channel_id=1, source_target_pairs={{0,1},{1,2},{2,3},{3,4},{4,5},{5,6},{6,7},{7,0},{8,9},{9,10},{10,1... | collective-permute-start | bytes 24584 | tf_op jit(solution)/shard_map/ppermute | solution.py:147
  173.8 6.3 %collective-permute-start.3 = (bf16[8,512]{1,0:T(8,128)(2,1)S(1)}, bf16[8,512]{1,0:T(8,128)(2,1)S(1)}, u32[]{:S(2)}, u32[]{:S(2)}) collective-permute-start(bf16[8,512]{1,0:T(8,128)(2,1)S(1)} %collective-permute-done.1), channel_id=1, source_target_pairs={{0,7},{1,0},{2,1},{3,2},{4,3},{5,4},{6,5},{7,6},{8,15},{9,8},{10,9... | collective-permute-start | bytes 24584 | tf_op jit(solution)/shard_map/ppermute | solution.py:150
  180.1 6.3 %collective-permute-start.4 = (bf16[8,512]{1,0:T(8,128)(2,1)S(1)}, bf16[8,512]{1,0:T(8,128)(2,1)S(1)}, u32[]{:S(2)}, u32[]{:S(2)}) collective-permute-start(bf16[8,512]{1,0:T(8,128)(2,1)S(1)} %collective-permute-done.2), channel_id=1, source_target_pairs={{0,1},{1,2},{2,3},{3,4},{4,5},{5,6},{6,7},{7,0},{8,9},{9,10},{10,1... | collective-permute-start | bytes 24584 | tf_op jit(solution)/shard_map/ppermute | solution.py:147
  180.1 6.3 %collective-permute-start.5 = (bf16[8,512]{1,0:T(8,128)(2,1)S(1)}, bf16[8,512]{1,0:T(8,128)(2,1)S(1)}, u32[]{:S(2)}, u32[]{:S(2)}) collective-permute-start(bf16[8,512]{1,0:T(8,128)(2,1)S(1)} %collective-permute-done.3), channel_id=1, source_target_pairs={{0,7},{1,0},{2,1},{3,2},{4,3},{5,4},{6,5},{7,6},{8,15},{9,8},{10,9... | collective-permute-start | bytes 24584 | tf_op jit(solution)/shard_map/ppermute | solution.py:150
  186.5 6.3 %collective-permute-start.6 = (bf16[8,512]{1,0:T(8,128)(2,1)S(1)}, bf16[8,512]{1,0:T(8,128)(2,1)S(1)}, u32[]{:S(2)}, u32[]{:S(2)}) collective-permute-start(bf16[8,512]{1,0:T(8,128)(2,1)S(1)} %collective-permute-done.4), channel_id=1, source_target_pairs={{0,1},{1,2},{2,3},{3,4},{4,5},{5,6},{6,7},{7,0},{8,9},{9,10},{10,1... | collective-permute-start | bytes 24584 | tf_op jit(solution)/shard_map/ppermute | solution.py:147
  198.5 11.6 %all-to-all-start.3 = ((bf16[8,32,512]{2,1,0:T(8,128)(2,1)}), bf16[8,32,512]{2,1,0:T(8,128)(2,1)S(1)}, u32[]{:S(2)}, u32[]{:S(2)}) async-start(bf16[8,32,512]{2,1,0:T(8,128)(2,1)} %bitcast.6), calls=%async_computation.3 | async-start | bytes 524288 | tf_op jit(solution)/shard_map/all_to_all | solution.py:130
  201.9 198.3 %all-reduce.5.cloned.1.call-start = ((), (), s32[]{:S(2)}) async-start(), calls=%async_computation.6 | async-start | bytes 4194304 | tf_op jit(solution)/shard_map/psum | solution.py:183
  (1 other events, 4.0 us)
Sparse Core Ops, SparseCore 0:
  97.2 62.9 reduce-scatter.1
  267.1 133.0 all-reduce.4
